TPU v7x, 128 devices: a whole 4x4x4 slice. The times are simulated.
128 devices in a mesh: row: 8 (over y, core), col: 16 (over z, x).
Axes of the slice: x: 4, y: 4, z: 4, core: 2. Of those that a mesh axis runs over, the one named last changes fastest.
Arguments:
- sigma_top: float32 [6144, 6144], P('row', 'col')
- factor_cross: float32 [6144, 6144], P('row', 'col'), may hold values from -0.078125 to 0.078125
- factor_inverse: float32 [6144, 6144], P('row', 'col')
- block_inverse: float32 [6144, 6144], P('row', 'col')
- ancestors: int32 [12], replicated, may hold values from 0 to 23, as said below
Outputs:
- sigma_cross: float32 [6144, 6144], P('row', 'col')
- sigma_child: float32 [6144, 6144], P('row', 'col')
Inputs may be any that keep to these rules, and one draw needn't show every extreme that they name: `ancestors`: 12 distinct block numbers; block 0 and block 23 are always among them.
All inputs are finite; a program needn't handle non-finite values.
Results may differ from a plain program's by a relative error of at most 0.000078.
Values sent between devices are 32-bit elements; how exact they have to be, the bound alone decides.
No kernel may reach another device: no remote copies, remote signals or barrier semaphores. Data moves between devices by JAX's collectives and lax.ppermute only.
A program may use at most 128 MiB of HBM per device.

v0:
```python
import jax
import jax.numpy as jnp
from jax import lax
from jax.sharding import PartitionSpec as P

BLK = 256


def transposed_rows(gathered, right_side):
    return lax.dot_general(
        gathered,
        right_side,
        (((0,), (0,)), ((), ())),
        precision=lax.Precision.HIGHEST,
        preferred_element_type=jnp.float32,
    )


def per_device(sigma_top, factor_cross, factor_inverse, block_inverse, ancestors):
    height = sigma_top.shape[0]
    first_row = lax.axis_index("row") * height
    blocks = (first_row + lax.iota(jnp.int32, height)) // BLK
    living = jnp.any(blocks[:, None] == ancestors[None, :], axis=1)
    masked = jnp.where(living[:, None], factor_cross, jnp.float32(0.0))
    inverse_strip = lax.all_gather(factor_inverse, "row", axis=0, tiled=True)
    rows_used = inverse_strip
    update = jnp.dot(
        lax.all_gather(masked, "col", axis=1, tiled=True),
        rows_used,
        precision=lax.Precision.HIGHEST,
        preferred_element_type=jnp.float32,
    )
    update_strip = lax.all_gather(update, "row", axis=0, tiled=True)
    rows_used = update_strip
    product = jnp.dot(
        lax.all_gather(sigma_top, "col", axis=1, tiled=True),
        rows_used,
        precision=lax.Precision.HIGHEST,
        preferred_element_type=jnp.float32,
    )
    sigma_cross = jnp.where(living[:, None], -product, jnp.float32(0.0))
    gathered = lax.all_gather(sigma_cross, "col", axis=1, tiled=True)
    correction = lax.psum_scatter(
        transposed_rows(gathered, update), "row", scatter_dimension=0, tiled=True
    )
    sigma_child = block_inverse - correction
    return (sigma_cross, sigma_child)


def solution(mesh):
    return jax.shard_map(
        per_device,
        mesh=mesh,
        in_specs=(P("row", "col"), P("row", "col"), P("row", "col"), P("row", "col"), P()),
        out_specs=(P("row", "col"), P("row", "col")),
        check_vma=False,
    )
```

profile of v0, /device:TPU:1, one launch (start us, length us, event | category | flops | bytes accessed | tf_op | source)
XLA Modules:
  0.0 643.4 jit_solution(8413906918570889155)
XLA Ops:
  7.2 0.0 all-gather.8.cloned.1.call-start
  7.2 0.7 all-gather.8.cloned.1.call-update
  7.9 0.0 all-gather.6.cloned.1.call-start
  8.0 0.7 compare_reduce_fusion
  8.7 2.5 broadcast_select_fusion
  11.2 0.0 all-gather.6.cloned.1.call-update
  11.2 0.0 all-gather.12.cloned.1.call-start
  11.2 0.7 all-gather.12.cloned.1.call-update
  11.9 0.0 all-gather.10.cloned.1.call-start
  12.0 55.5 %all-gather.8.cloned.1.call-done = f32[6144,384]{1,0:T(8,128)} async-done(((f32[768,384]{1,0:T(8,128)}), f32[6144,384]{1,0:T(8,128)}) %all-gather.8.cloned.1.call-update) | async-done | bytes 9437200 | tf_op jit(solution)/shard_map/all_gather | solution.py:25
  67.5 124.8 %all-gather.6.cloned.1.call-done = f32[768,6144]{1,0:T(8,128)} async-done(((f32[768,384]{1,0:T(8,128)}), f32[768,6144]{1,0:T(8,128)}) %all-gather.6.cloned.1.call-update) | async-done | bytes 18874384 | tf_op jit(solution)/shard_map/all_gather | solution.py:28
  192.3 34.1 %fusion.5 = f32[768,384]{1,0:T(8,128)} fusion(f32[768,6144]{1,0:T(8,128)} %all-gather.6.cloned.1.call-done, f32[6144,384]{1,0:T(8,128)} %all-gather.8.cloned.1.call-done), kind=kOutput, calls=%fused_computation.14 | convolution fusion | flops 21743271936 | bytes 29491200 | tf_op jit(solution)/shard_map/dot_general | solution.py:27
  226.4 0.0 all-gather.10.cloned.1.call-update
  226.4 0.0 copy-start
  226.4 0.2 all-gather.14.cloned.1.call-start
  226.6 89.7 %all-gather.12.cloned.1.call-done = f32[768,6144]{1,0:T(8,128)} async-done(((f32[768,384]{1,0:T(8,128)}), f32[768,6144]{1,0:T(8,128)}) %all-gather.12.cloned.1.call-update) | async-done | bytes 18874384 | tf_op jit(solution)/shard_map/all_gather | solution.py:36
  316.3 56.3 %all-gather.10.cloned.1.call-done = f32[6144,384]{1,0:T(8,128)} async-done(((f32[768,384]{1,0:T(8,128)}), f32[6144,384]{1,0:T(8,128)}) %all-gather.10.cloned.1.call-update) | async-done | bytes 9437200 | tf_op jit(solution)/shard_map/all_gather | solution.py:33
  372.6 48.7 %fusion.1 = f32[768,384]{0,1:T(8,128)} fusion(f32[6144,384]{1,0:T(8,128)} %all-gather.10.cloned.1.call-done, f32[768,6144]{1,0:T(8,128)} %all-gather.12.cloned.1.call-done, pred[768]{0:T(1024)(128)(4,1)S(1)} %compare_reduce_fusion), kind=kOutput, calls=%fused_computation.2 | convolution fusion | flops 21743861760 | bytes 29491968 | tf_op jit(solution)/shard_map/dot_general | solution.py:35
  421.3 0.0 all-gather.14.cloned.1.call-update
  421.3 0.3 reduce-scatter.2.cloned.1.call-start
  421.6 121.8 %all-gather.14.cloned.1.call-done = f32[768,6144]{0,1:T(8,128)} async-done(((f32[768,384]{0,1:T(8,128)}), f32[768,6144]{0,1:T(8,128)}) %all-gather.14.cloned.1.call-update) | async-done | bytes 18874384 | tf_op jit(solution)/shard_map/all_gather | solution.py:42
  543.4 0.0 copy-done
  543.4 34.0 %fusion.6 = f32[6144,384]{1,0:T(8,128)} fusion(f32[768,6144]{0,1:T(8,128)} %all-gather.14.cloned.1.call-done, f32[768,384]{1,0:T(8,128)S(1)} %copy-done), kind=kOutput, calls=%fused_computation.15 | convolution fusion | flops 21743271936 | bytes 29491200 | tf_op jit(solution)/shard_map/dot_general | solution.py:10
  577.5 0.0 copy-start.1
  577.5 0.0 copy-start.2
  577.5 0.0 reduce-scatter.2.cloned.1.call-update
  577.5 1.2 copy-done.1
  578.8 1.4 copy.8
  580.2 54.0 %reduce-scatter.2.cloned.1.call-done = f32[768,384]{1,0:T(8,128)} async-done(((f32[6144,384]{1,0:T(8,128)}), f32[768,384]{1,0:T(8,128)}) %reduce-scatter.2.cloned.1.call-update) | async-done | bytes 1179664 | tf_op jit(solution)/shard_map/reduce_scatter | solution.py:43
  634.2 0.0 copy-done.2
  634.2 2.4 sub.10
  (1 shorter events, 0.0 us)
Async XLA Ops:
  7.2 60.3 %all-gather.8.cloned.1.call-start = ((), (), s32[]{:S(2)}) async-start(), calls=%async_computation.2 | async-start | bytes 10616832 | tf_op jit(solution)/shard_map/all_gather | solution.py:25
  7.9 184.4 %all-gather.6.cloned.1.call-start = ((), (), s32[]{:S(2)}) async-start(), calls=%async_computation.1 | async-start | bytes 20054016 | tf_op jit(solution)/shard_map/all_gather | solution.py:28
  11.2 305.1 %all-gather.12.cloned.1.call-start = ((), (), s32[]{:S(2)}) async-start(), calls=%async_computation.4 | async-start | bytes 20054016 | tf_op jit(solution)/shard_map/all_gather | solution.py:36
  11.9 360.6 %all-gather.10.cloned.1.call-start = ((), (), s32[]{:S(2)}) async-start(), calls=%async_computation.3 | async-start | bytes 10616832 | tf_op jit(solution)/shard_map/all_gather | solution.py:33
  226.4 317.1 %copy-start = (f32[768,384]{1,0:T(8,128)S(1)}, f32[768,384]{1,0:T(8,128)}, u32[]{:S(2)}) copy-start(f32[768,384]{1,0:T(8,128)} %fusion.5) | copy-start | bytes 3538948
  226.4 317.0 %all-gather.14.cloned.1.call-start = ((), (), s32[]{:S(2)}) async-start(), calls=%async_computation.5 | async-start | bytes 20054016 | tf_op jit(solution)/shard_map/all_gather | solution.py:42
  421.3 212.8 %reduce-scatter.2.cloned.1.call-start = ((), (), s32[]{:S(2)}) async-start(), calls=%async_computation.6 | async-start | bytes 10616832 | tf_op jit(solution)/shard_map/reduce_scatter | solution.py:43
  577.5 1.3 copy-start.1
  577.5 56.7 %copy-start.2 = (f32[768,384]{1,0:T(8,128)S(1)}, f32[768,384]{1,0:T(8,128)}, u32[]{:S(2)}) copy-start(f32[768,384]{1,0:T(8,128)} %param.8) | copy-start | bytes 3538948
Sparse Core Ops, SparseCore 0:
  9.7 57.7 all-gather.7
  70.3 121.9 all-gather.5
  194.5 121.7 all-gather.11
  318.4 54.1 all-gather.9
  421.5 121.9 all-gather.13
  577.6 56.4 reduce-scatter.1
where the time goes:
time: 644 us; the launch traced here: 643 us
  waiting for transfers between devices  504 us (78%)
  matrix products  117 us (18%)
  between operations  14.1 us (2%)
    all_gather x1, waiting for transfers between devices, per_device(): lax.all_gather(masked, 'col', axis=1, tiled=True)  125 us
    all_gather x1, waiting for transfers between devices, per_device(): gathered = lax.all_gather(sigma_cross, 'col', axis=1, tiled=True)  122 us
    all_gather x1, waiting for transfers between devices, per_device(): lax.all_gather(sigma_top, 'col', axis=1, tiled=True)  89.7 us
    all_gather x1, waiting for transfers between devices, per_device(): update_strip = lax.all_gather(update, 'row', axis=0, tiled=True)  56.3 us
    all_gather x1, waiting for transfers between devices, per_device(): inverse_strip = lax.all_gather(factor_inverse, 'row', axis=0, tiled=True)  55.5 us
    reduce_scatter x1, waiting for transfers between devices, per_device(): lax.psum_scatter(transposed_rows(gathered, update), 'row', scatter_dimens...  54 us
    dot_general x1, matrix products, per_device(): jnp.dot(lax.all_gather(sigma_top, 'col', axis=1, tiled=True), rows_used,...  48.7 us
    dot_general x1, matrix products, per_device(): jnp.dot(lax.all_gather(masked, 'col', axis=1, tiled=True), rows_used, pre...  34.1 us
  transfers between devices with their start and end apart: 6, of which 6 were waited for; matrix products, arithmetic and copies ran while one was open for 6% of the time, Pallas kernels for 0%

commit v1 on v0

--- a/solution.py
+++ b/solution.py
@@ -4,6 +4,14 @@
 from jax.sharding import PartitionSpec as P
 
 BLK = 256
+
+
+def see_wires(obj):
+    frames = []
+    for _ in range(lax.axis_size("col")):
+        frames.append(obj)
+    top = jnp.concatenate(lax.all_to_all(jnp.stack(frames), "col", 0, 0), 1)
+    return top
 
 
 def transposed_rows(gathered, right_side):
@@ -33,7 +41,7 @@
     update_strip = lax.all_gather(update, "row", axis=0, tiled=True)
     rows_used = update_strip
     product = jnp.dot(
-        lax.all_gather(sigma_top, "col", axis=1, tiled=True),
+        see_wires(sigma_top),
         rows_used,
         precision=lax.Precision.HIGHEST,
         preferred_element_type=jnp.float32,

time: 644 us -> 739 us (1.15)
  waiting for transfers between devices: 504 us -> 601 us
  matrix products: 117 us -> 96.4 us
  local copies, waits for them, and re-layouts: 2.64 us -> 12.6 us
  starting transfers between devices: 0.64 us -> 9.49 us
    all_gather x1, waiting for transfers between devices: 125 us -> 321 us  [per_device(): lax.all_gather(masked, 'col', axis=1, tiled=True)]
    all_gather x1 -> x0, waiting for transfers between devices: 89.7 us -> none  [per_device(): lax.all_gather(sigma_top, 'col', axis=1, tiled=True)]
    dot_general x1, matrix products: 48.7 us -> 28.2 us  [per_device(): jnp.dot(see_wires(sigma_top), rows_used, precision=lax.Precision.HIGHEST,...]
    all_gather x1, waiting for transfers between devices: 55.5 us -> 37.4 us  [per_device(): inverse_strip = lax.all_gather(factor_inverse, 'row', axis=0, tiled=True)]
    all_gather x1, waiting for transfers between devices: 56.3 us -> 66.2 us  [per_device(): update_strip = lax.all_gather(update, 'row', axis=0, tiled=True)]
    all_to_all x0 -> x1, starting transfers between devices: none -> 8.89 us  [see_wires(): top = jnp.concatenate(lax.all_to_all(jnp.stack(frames), 'col', 0, 0), 1)]
    another operation x0 -> x1, local copies, waits for them, and re-layouts: none -> 8.3 us  [see_wires(): top = jnp.concatenate(lax.all_to_all(jnp.stack(frames), 'col', 0, 0), 1)]
  transfers between devices with their start and end apart: 6 -> 6, of which waited for: 6 -> 5; matrix products, arithmetic and copies ran while one was open for 6% -> 7% of each run, Pallas kernels for 0% -> 0%
where the time goes in v1:
time: 739 us
  waiting for transfers between devices  601 us (81%)
  matrix products  96.4 us (13%)
  between operations  13.8 us (2%)
  local copies, waits for them, and re-layouts  12.6 us (2%)
  starting transfers between devices  9.49 us (1%)
    all_gather x1, waiting for transfers between devices, per_device(): lax.all_gather(masked, 'col', axis=1, tiled=True)  321 us
    all_gather x1, waiting for transfers between devices, per_device(): gathered = lax.all_gather(sigma_cross, 'col', axis=1, tiled=True)  122 us
    all_gather x1, waiting for transfers between devices, per_device(): update_strip = lax.all_gather(update, 'row', axis=0, tiled=True)  66.2 us
    reduce_scatter x1, waiting for transfers between devices, per_device(): lax.psum_scatter(transposed_rows(gathered, update), 'row', scatter_dimens...  54 us
    all_gather x1, waiting for transfers between devices, per_device(): inverse_strip = lax.all_gather(factor_inverse, 'row', axis=0, tiled=True)  37.4 us
    dot_general x1, matrix products, per_device(): jnp.dot(lax.all_gather(masked, 'col', axis=1, tiled=True), rows_used, pre...  34.1 us
    dot_general x1, matrix products, transposed_rows(): lax.dot_general(gathered, right_side, (((0,), (0,)), ((), ())), precision...  34 us
    dot_general x1, matrix products, per_device(): jnp.dot(see_wires(sigma_top), rows_used, precision=lax.Precision.HIGHEST,...  28.2 us
  transfers between devices with their start and end apart: 6, of which 5 were waited for; matrix products, arithmetic and copies ran while one was open for 7% of the time, Pallas kernels for 0%

profile of v1, /device:TPU:1, one launch (start us, length us, event | category | flops | bytes accessed | tf_op | source)
XLA Modules:
  0.0 739.1 jit_solution(17816218260355831227)
XLA Ops:
  7.2 0.0 all-gather.7.cloned.1.call-start
  7.2 0.7 all-gather.7.cloned.1.call-update
  7.9 0.0 all-gather.5.cloned.1.call-start
  8.0 0.7 compare_reduce_fusion
  8.7 2.5 broadcast_select_fusion
  11.2 0.0 all-gather.5.cloned.1.call-update
  11.2 1.6 copy.10
  12.8 8.3 %stack.2 = f32[16,768,384]{1,2,0:T(8,128)} broadcast(f32[768,384]{0,1:T(8,128)S(1)} %copy.10), dimensions={1,2} | broadcast | bytes 20054016 | tf_op jit(solution)/shard_map/stack | solution.py:13
  21.1 8.9 %all-to-all-start = ((f32[16,768,384]{1,2,0:T(8,128)}), f32[16,768,384]{1,2,0:T(8,128)}, u32[]{:S(2)}, u32[]{:S(2)}) async-start(f32[16,768,384]{1,2,0:T(8,128)} %stack.2), calls=%async_computation | async-start | bytes 37748736 | tf_op jit(solution)/shard_map/all_to_all | solution.py:13
  30.0 0.0 all-gather.9.cloned.1.call-start
  30.1 37.4 %all-gather.7.cloned.1.call-done = f32[6144,384]{1,0:T(8,128)} async-done(((f32[768,384]{1,0:T(8,128)}), f32[6144,384]{1,0:T(8,128)}) %all-gather.7.cloned.1.call-update) | async-done | bytes 9437200 | tf_op jit(solution)/shard_map/all_gather | solution.py:33
  67.5 321.1 %all-gather.5.cloned.1.call-done = f32[768,6144]{1,0:T(8,128)} async-done(((f32[768,384]{1,0:T(8,128)}), f32[768,6144]{1,0:T(8,128)}) %all-gather.5.cloned.1.call-update) | async-done | bytes 18874384 | tf_op jit(solution)/shard_map/all_gather | solution.py:36
  388.6 34.1 %fusion.5 = f32[768,384]{1,0:T(8,128)} fusion(f32[768,6144]{1,0:T(8,128)} %all-gather.5.cloned.1.call-done, f32[6144,384]{1,0:T(8,128)} %all-gather.7.cloned.1.call-done), kind=kOutput, calls=%fused_computation.14 | convolution fusion | flops 21743271936 | bytes 29491200 | tf_op jit(solution)/shard_map/dot_general | solution.py:35
  422.7 0.0 all-gather.9.cloned.1.call-update
  422.7 0.2 all-gather.11.cloned.1.call-start
  422.9 0.0 all-to-all-done
  423.0 66.2 %all-gather.9.cloned.1.call-done = f32[6144,384]{1,0:T(8,128)} async-done(((f32[768,384]{1,0:T(8,128)}), f32[6144,384]{1,0:T(8,128)}) %all-gather.9.cloned.1.call-update) | async-done | bytes 9437200 | tf_op jit(solution)/shard_map/all_gather | solution.py:41
  489.1 0.0 copy-start
  489.1 28.2 %fusion.1 = f32[768,384]{0,1:T(8,128)} fusion(f32[6144,384]{1,0:T(8,128)} %all-gather.9.cloned.1.call-done, f32[768,6144]{0,1:T(8,128)} %bitcast.1, pred[768]{0:T(1024)(128)(4,1)S(1)} %compare_reduce_fusion), kind=kOutput, calls=%fused_computation.2 | convolution fusion | flops 21743861760 | bytes 29491968 | tf_op jit(solution)/shard_map/dot_general | solution.py:43
  517.4 0.0 all-gather.11.cloned.1.call-update
  517.4 0.3 reduce-scatter.2.cloned.1.call-start
  517.7 121.8 %all-gather.11.cloned.1.call-done = f32[768,6144]{0,1:T(8,128)} async-done(((f32[768,384]{0,1:T(8,128)}), f32[768,6144]{0,1:T(8,128)}) %all-gather.11.cloned.1.call-update) | async-done | bytes 18874384 | tf_op jit(solution)/shard_map/all_gather | solution.py:50
  639.5 0.0 copy-done
  639.5 34.0 %fusion.6 = f32[6144,384]{1,0:T(8,128)} fusion(f32[768,6144]{0,1:T(8,128)} %all-gather.11.cloned.1.call-done, f32[768,384]{1,0:T(8,128)S(1)} %copy-done), kind=kOutput, calls=%fused_computation.15 | convolution fusion | flops 21743271936 | bytes 29491200 | tf_op jit(solution)/shard_map/dot_general | solution.py:18
  673.5 0.0 copy-start.1
  673.5 0.0 copy-start.2
  673.5 0.0 reduce-scatter.2.cloned.1.call-update
  673.6 1.2 copy-done.1
  674.8 1.4 copy.11
  676.2 54.0 %reduce-scatter.2.cloned.1.call-done = f32[768,384]{1,0:T(8,128)} async-done(((f32[6144,384]{1,0:T(8,128)}), f32[768,384]{1,0:T(8,128)}) %reduce-scatter.2.cloned.1.call-update) | async-done | bytes 1179664 | tf_op jit(solution)/shard_map/reduce_scatter | solution.py:51
  730.2 0.0 copy-done.2
  730.2 2.4 sub.10
  (1 shorter events, 0.0 us)
Async XLA Ops:
  7.2 60.3 %all-gather.7.cloned.1.call-start = ((), (), s32[]{:S(2)}) async-start(), calls=%async_computation.3 | async-start | bytes 10616832 | tf_op jit(solution)/shard_map/all_gather | solution.py:33
  7.9 380.7 %all-gather.5.cloned.1.call-start = ((), (), s32[]{:S(2)}) async-start(), calls=%async_computation.2 | async-start | bytes 20054016 | tf_op jit(solution)/shard_map/all_gather | solution.py:36
  21.1 401.8 %all-to-all-start = ((f32[16,768,384]{1,2,0:T(8,128)}), f32[16,768,384]{1,2,0:T(8,128)}, u32[]{:S(2)}, u32[]{:S(2)}) async-start(f32[16,768,384]{1,2,0:T(8,128)} %stack.2), calls=%async_computation | async-start | bytes 37748736 | tf_op jit(solution)/shard_map/all_to_all | solution.py:13
  30.0 459.1 %all-gather.9.cloned.1.call-start = ((), (), s32[]{:S(2)}) async-start(), calls=%async_computation.4 | async-start | bytes 10616832 | tf_op jit(solution)/shard_map/all_gather | solution.py:41
  422.7 216.8 %all-gather.11.cloned.1.call-start = ((), (), s32[]{:S(2)}) async-start(), calls=%async_computation.5 | async-start | bytes 20054016 | tf_op jit(solution)/shard_map/all_gather | solution.py:50
  489.1 150.4 %copy-start = (f32[768,384]{1,0:T(8,128)S(1)}, f32[768,384]{1,0:T(8,128)}, u32[]{:S(2)}) copy-start(f32[768,384]{1,0:T(8,128)} %fusion.5) | copy-start | bytes 3538948
  517.4 212.8 %reduce-scatter.2.cloned.1.call-start = ((), (), s32[]{:S(2)}) async-start(), calls=%async_computation.6 | async-start | bytes 10616832 | tf_op jit(solution)/shard_map/reduce_scatter | solution.py:51
  673.5 1.3 copy-start.1
  673.5 56.7 %copy-start.2 = (f32[768,384]{1,0:T(8,128)S(1)}, f32[768,384]{1,0:T(8,128)}, u32[]{:S(2)}) copy-start(f32[768,384]{1,0:T(8,128)} %param.8) | copy-start | bytes 3538948
Sparse Core Ops, SparseCore 0:
  9.7 57.7 all-gather.6
  70.3 318.3 all-gather.4
  422.8 66.2 all-gather.8
  517.5 121.9 all-gather.10
  673.7 56.4 reduce-scatter.1
